TPU v7x, 32 devices: a whole 2x2x4 slice. The times are simulated.
32 devices in a mesh: dp: 8 (over z, x), rep: 4 (over y, core).
Axes of the slice: x: 2, y: 2, z: 4, core: 2. Of those that a mesh axis runs over, the one named last changes fastest.
Arguments:
- images: bfloat16 [128, 14, 14, 1024], P(('dp', 'rep')), may hold values from -18 to 18, as said below
- out_grad: bfloat16 [128, 14, 14, 1024], P(('dp', 'rep')), may hold values from -18 to 18, as said below
- reduce_weight: float32 [1024, 256], P('dp'), may hold values from -0.1875 to 0.1875
- reduce_moment: float32 [1024, 256], P('dp'), may hold values from -224 to 224
- reduce_second: float32 [1024, 256], P('dp'), may hold values from 100.352 to 401.408
- conv_weight: float32 [2304, 256], P('dp'), may hold values from -0.1875 to 0.1875
- conv_moment: float32 [2304, 256], P('dp'), may hold values from -128 to 128
- conv_second: float32 [2304, 256], P('dp'), may hold values from 50.176 to 200.704
- squeeze_weight: float32 [256, 128], P('dp'), may hold values from -0.375 to 0.375
- squeeze_moment: float32 [256, 128], P('dp'), may hold values from -56 to 56
- squeeze_second: float32 [256, 128], P('dp'), may hold values from 6.272 to 25.088
- expand_weight: float32 [128, 512], P('dp'), may hold values from -1.5 to 1.5
- expand_moment: float32 [128, 512], P('dp'), may hold values from -56 to 56
- expand_second: float32 [128, 512], P('dp'), may hold values from 6.272 to 25.088
- project_weight: float32 [256, 1024], P('dp'), may hold values from -0.375 to 0.375
- project_moment: float32 [256, 1024], P('dp'), may hold values from -112 to 112
- project_second: float32 [256, 1024], P('dp'), may hold values from 30.1056 to 120.4224
- norm_params: float32 [4352], P('dp'), may hold values from -0.5 to 1.4, as said below
- norm_moment: float32 [4352], P('dp'), may hold values from -128 to 128
- norm_second: float32 [4352], P('dp'), may hold values from 35.1232 to 145.5104
Outputs:
- block_out: bfloat16 [128, 14, 14, 1024], P(('dp', 'rep'))
- images_grad: float32 [128, 14, 14, 1024], P(('dp', 'rep'))
- new_reduce_weight: float32 [1024, 256], P('dp')
- new_reduce_moment: float32 [1024, 256], P('dp')
- new_reduce_second: float32 [1024, 256], P('dp')
- new_conv_weight: float32 [2304, 256], P('dp')
- new_conv_moment: float32 [2304, 256], P('dp')
- new_conv_second: float32 [2304, 256], P('dp')
- new_squeeze_weight: float32 [256, 128], P('dp')
- new_squeeze_moment: float32 [256, 128], P('dp')
- new_squeeze_second: float32 [256, 128], P('dp')
- new_expand_weight: float32 [128, 512], P('dp')
- new_expand_moment: float32 [128, 512], P('dp')
- new_expand_second: float32 [128, 512], P('dp')
- new_project_weight: float32 [256, 1024], P('dp')
- new_project_moment: float32 [256, 1024], P('dp')
- new_project_second: float32 [256, 1024], P('dp')
- new_norm_params: float32 [4352], P('dp')
- new_norm_moment: float32 [4352], P('dp')
- new_norm_second: float32 [4352], P('dp')
Inputs may be any that keep to these rules, and one draw needn't show every extreme that they name: `images`: entries drawn independently. `out_grad`: entries drawn independently. `norm_params`: gains lie near one, biases near zero.
All inputs are finite; a program needn't handle non-finite values.
Results may differ from a plain program's by a relative error of at most 0.0055.
The roundings to bfloat16 on the way count: a program that leaves them out, or rounds other values in their place, can miss the bound.
Values may be sent and summed in bfloat16 or wider, within the bound.
A program may use at most 128 MiB of HBM per device.

v0:
```python
import functools
import jax
import jax.numpy as jnp
from jax import lax
from jax.experimental import pallas as pl
from jax.experimental.pallas import tpu as pltpu
from jax.sharding import PartitionSpec as P

CHANNELS = 1024
BOTTLE = 256
INNER = 128
RADIX = 2
SIDE = 14
MICRO = 2
STEP = 10


EPSILON = 1e-05
PRECISE = lax.Precision.HIGHEST
BETA_ONE = 0.9
BETA_TWO = 0.999
ADAM_EPSILON = 1e-08
DECAY = 0.01
NORM_RATE = 0.8
ROWS = 4 * SIDE * SIDE
NORM_WIDTH = 4352


def split_params(packed):
    widths = (
        BOTTLE,
        BOTTLE,
        RADIX * BOTTLE,
        RADIX * BOTTLE,
        INNER,
        INNER,
        RADIX * BOTTLE,
        CHANNELS,
        CHANNELS,
    )
    pieces = []
    offset = 0
    for segment in widths:
        pieces.append(lax.slice_in_dim(packed, offset, offset + segment))
        offset = offset + segment
    return pieces


def silu_slope(values):
    logistic = jax.nn.sigmoid(values)
    return logistic * (1.0 + values * (1.0 - logistic))


def norm_forward(values, gain, bias, count):
    flat = values.reshape(-1, values.shape[-1])
    total, square = lax.psum((jnp.sum(flat, axis=0), jnp.sum(flat * flat, axis=0)), ("dp", "rep"))
    center = total / count
    scale = lax.rsqrt(square / count - center * center + EPSILON)
    normed = (values - center) * scale
    return (normed * gain + bias, normed, scale)


def norm_backward(upstream, normed, scale, gain, count):
    flat_up = upstream.reshape(-1, upstream.shape[-1])
    flat_norm = normed.reshape(-1, normed.shape[-1])
    bias_sum, gain_sum = lax.psum(
        (jnp.sum(flat_up, axis=0), jnp.sum(flat_up * flat_norm, axis=0)), ("dp", "rep")
    )
    downstream = gain * scale * (upstream - bias_sum / count - normed * (gain_sum / count))
    return (downstream, gain_sum, bias_sum)


def patches(active):
    padded = jnp.pad(active, ((0, 0), (1, 1), (1, 1), (0, 0), (0, 0)))
    shifted = [
        padded[:, down_step : down_step + SIDE, side_step : side_step + SIDE]
        for down_step in range(3)
        for side_step in range(3)
    ]
    return jnp.stack(shifted, axis=4)


def unpatch(columns):
    total = jnp.zeros(
        (columns.shape[0], SIDE + 2, SIDE + 2, columns.shape[3], columns.shape[5]), jnp.float32
    )
    for down_step in range(3):
        for side_step in range(3):
            piece = columns[:, :, :, :, 3 * down_step + side_step]
            total = total + jnp.pad(
                piece,
                ((0, 0), (down_step, 2 - down_step), (side_step, 2 - side_step), (0, 0), (0, 0)),
            )
    return total[:, 1 : SIDE + 1, 1 : SIDE + 1]


def adamw(param, moment, second, gradient, rate, decay):
    moment_new = BETA_ONE * moment + (1.0 - BETA_ONE) * gradient
    second_new = BETA_TWO * second + (1.0 - BETA_TWO) * gradient * gradient
    ratio = (
        moment_new
        / (1.0 - BETA_ONE**STEP)
        / (jnp.sqrt(second_new / (1.0 - BETA_TWO**STEP)) + ADAM_EPSILON)
    )
    return (param - rate * (ratio + decay * param), moment_new, second_new)


def per_device(
    images,
    out_grad,
    reduce_weight,
    reduce_moment,
    reduce_second,
    conv_weight,
    conv_moment,
    conv_second,
    squeeze_weight,
    squeeze_moment,
    squeeze_second,
    expand_weight,
    expand_moment,
    expand_second,
    project_weight,
    project_moment,
    project_second,
    norm_params,
    norm_moment,
    norm_second,
):
    bf16 = jnp.bfloat16
    low_reduce = reduce_weight.astype(bf16)
    low_conv = conv_weight.astype(bf16)
    low_squeeze = squeeze_weight.astype(bf16)
    low_expand = expand_weight.astype(bf16)
    low_project = project_weight.astype(bf16)
    low_norm = norm_params.astype(bf16)
    devices = lax.axis_size("dp") * lax.axis_size("rep")
    per_batch = images.shape[0] // MICRO
    pixel_count = float(per_batch * SIDE * SIDE * devices)
    image_count = float(per_batch * devices)
    group_in = BOTTLE // RADIX
    grad_first = jnp.zeros((CHANNELS, BOTTLE), jnp.float32)
    grad_conv = jnp.zeros((RADIX, 9 * group_in, BOTTLE), jnp.float32)
    grad_squeeze = jnp.zeros((BOTTLE, INNER), jnp.float32)
    grad_expand = jnp.zeros((INNER, RADIX * BOTTLE), jnp.float32)
    grad_last = jnp.zeros((BOTTLE, CHANNELS), jnp.float32)
    grad_norms = jnp.zeros(
        (2 * BOTTLE + 3 * RADIX * BOTTLE + 2 * INNER + 2 * CHANNELS,), jnp.float32
    )
    outputs = []
    input_grads = []
    for number in range(MICRO):
        forward_set = (
            lax.all_gather(low_reduce, "dp", axis=0, tiled=True),
            lax.all_gather(low_conv, "dp", axis=0, tiled=True),
            lax.all_gather(low_squeeze, "dp", axis=0, tiled=True),
            lax.all_gather(low_expand, "dp", axis=0, tiled=True),
            lax.all_gather(low_project, "dp", axis=0, tiled=True),
            lax.all_gather(low_norm, "dp", axis=0, tiled=True),
        )
        first, conv, squeeze, expand, last, packed = forward_set
        (
            gain_one,
            bias_one,
            gain_two,
            bias_two,
            gain_pool,
            bias_pool,
            bias_expand,
            gain_three,
            bias_three,
        ) = split_params(packed.astype(jnp.float32))
        batched = images[number * per_batch : (number + 1) * per_batch]
        cotangent = out_grad[number * per_batch : (number + 1) * per_batch]
        reduced = jnp.einsum("nhwc,cb->nhwb", batched, first, preferred_element_type=jnp.float32)
        norm_one, normed_one, scale_one = norm_forward(reduced, gain_one, bias_one, pixel_count)
        active = jax.nn.silu(norm_one).astype(bf16)
        columns = patches(active.reshape(per_batch, SIDE, SIDE, RADIX, group_in)).reshape(
            per_batch * SIDE * SIDE, RADIX, 9 * group_in
        )
        conv_grouped = conv.reshape(RADIX, 9 * group_in, BOTTLE)
        widened = jnp.einsum(
            "prk,rko->pro", columns, conv_grouped, preferred_element_type=jnp.float32
        )
        widened = widened.reshape(per_batch, SIDE, SIDE, RADIX * BOTTLE)
        norm_two, normed_two, scale_two = norm_forward(widened, gain_two, bias_two, pixel_count)
        splits = jax.nn.silu(norm_two).reshape(per_batch, SIDE, SIDE, RADIX, BOTTLE)
        pooled = jnp.sum(jnp.sum(splits, axis=3), axis=(1, 2)) / (SIDE * SIDE)
        squeeze_float = squeeze.astype(jnp.float32)
        expand_float = expand.astype(jnp.float32)
        pre_pool = jnp.dot(pooled, squeeze_float, precision=PRECISE)
        norm_pool, normed_pool, scale_pool = norm_forward(
            pre_pool, gain_pool, bias_pool, image_count
        )
        hidden = jax.nn.silu(norm_pool)
        logits = (jnp.dot(hidden, expand_float, precision=PRECISE) + bias_expand).reshape(
            per_batch, RADIX, BOTTLE
        )
        attention = jax.nn.softmax(logits, axis=1)
        mixed = jnp.sum(splits * attention[:, None, None], axis=3).astype(bf16)
        projected = jnp.einsum("nhwb,bc->nhwc", mixed, last, preferred_element_type=jnp.float32)
        norm_three, normed_three, scale_three = norm_forward(
            projected, gain_three, bias_three, pixel_count
        )
        summed = batched.astype(jnp.float32) + norm_three
        outputs.append(jax.nn.silu(summed).astype(bf16))
        backward_set = (
            lax.all_gather(low_reduce, "dp", axis=0, tiled=True),
            lax.all_gather(low_conv, "dp", axis=0, tiled=True),
            lax.all_gather(low_squeeze, "dp", axis=0, tiled=True),
            lax.all_gather(low_expand, "dp", axis=0, tiled=True),
            lax.all_gather(low_project, "dp", axis=0, tiled=True),
            lax.all_gather(low_norm, "dp", axis=0, tiled=True),
        )
        first, conv, squeeze, expand, last, packed = backward_set
        gains_back = split_params(packed.astype(jnp.float32))
        conv_grouped = conv.reshape(RADIX, 9 * group_in, BOTTLE)
        expand_float = expand.astype(jnp.float32)
        squeeze_float = squeeze.astype(jnp.float32)
        upstream = cotangent.astype(jnp.float32) * silu_slope(summed)
        d_projected, gain_three_grad, bias_three_grad = norm_backward(
            upstream, normed_three, scale_three, gains_back[7], pixel_count
        )
        d_projected_low = d_projected.astype(bf16)
        grad_last = grad_last + jnp.einsum(
            "nhwb,nhwc->bc", mixed, d_projected_low, preferred_element_type=jnp.float32
        )
        d_mixed = jnp.einsum(
            "nhwc,bc->nhwb", d_projected_low, last, preferred_element_type=jnp.float32
        )
        d_splits = d_mixed[:, :, :, None] * attention[:, None, None]
        d_attention = jnp.sum(d_mixed[:, :, :, None] * splits, axis=(1, 2))
        d_logits = attention * (
            d_attention - jnp.sum(attention * d_attention, axis=1, keepdims=True)
        )
        flat_logits = d_logits.reshape(per_batch, RADIX * BOTTLE)
        grad_expand = grad_expand + jnp.dot(hidden.T, flat_logits, precision=PRECISE)
        d_hidden = jnp.dot(flat_logits, expand_float.T, precision=PRECISE)
        d_pool_norm = d_hidden * silu_slope(norm_pool)
        pool_bias_sum, pool_gain_sum, expand_bias_sum = lax.psum(
            (
                jnp.sum(d_pool_norm, axis=0),
                jnp.sum(d_pool_norm * normed_pool, axis=0),
                jnp.sum(flat_logits, axis=0),
            ),
            ("dp", "rep"),
        )
        d_pre_pool = (
            gains_back[4]
            * scale_pool
            * (
                d_pool_norm
                - pool_bias_sum / image_count
                - normed_pool * (pool_gain_sum / image_count)
            )
        )
        grad_squeeze = grad_squeeze + jnp.dot(pooled.T, d_pre_pool, precision=PRECISE)
        d_pooled = jnp.dot(d_pre_pool, squeeze_float.T, precision=PRECISE)
        d_splits = d_splits + (d_pooled / (SIDE * SIDE))[:, None, None, None, :]
        d_norm_two = d_splits.reshape(per_batch, SIDE, SIDE, RADIX * BOTTLE) * silu_slope(norm_two)
        d_widened, gain_two_grad, bias_two_grad = norm_backward(
            d_norm_two, normed_two, scale_two, gains_back[2], pixel_count
        )
        d_widened_low = d_widened.astype(bf16).reshape(per_batch * SIDE * SIDE, RADIX, BOTTLE)
        grad_conv = grad_conv + jnp.einsum(
            "prk,pro->rko", columns, d_widened_low, preferred_element_type=jnp.float32
        )
        d_columns = jnp.einsum(
            "pro,rko->prk", d_widened_low, conv_grouped, preferred_element_type=jnp.float32
        )
        d_active = unpatch(d_columns.reshape(per_batch, SIDE, SIDE, RADIX, 9, group_in)).reshape(
            per_batch, SIDE, SIDE, BOTTLE
        )
        d_norm_one = d_active * silu_slope(norm_one)
        d_reduced, gain_one_grad, bias_one_grad = norm_backward(
            d_norm_one, normed_one, scale_one, gains_back[0], pixel_count
        )
        d_reduced_low = d_reduced.astype(bf16)
        grad_first = grad_first + jnp.einsum(
            "nhwc,nhwb->cb", batched, d_reduced_low, preferred_element_type=jnp.float32
        )
        input_grads.append(
            upstream
            + jnp.einsum("nhwb,cb->nhwc", d_reduced_low, first, preferred_element_type=jnp.float32)
        )
        grad_norms = grad_norms + jnp.concatenate(
            [
                gain_one_grad,
                bias_one_grad,
                gain_two_grad,
                bias_two_grad,
                pool_gain_sum,
                pool_bias_sum,
                expand_bias_sum,
                gain_three_grad,
                bias_three_grad,
            ]
        )
    grad_conv = grad_conv.reshape(9 * BOTTLE, BOTTLE)
    partial_value = (
        lax.psum_scatter(grad_first, "dp", scatter_dimension=0, tiled=True),
        lax.psum_scatter(grad_conv, "dp", scatter_dimension=0, tiled=True),
        lax.psum_scatter(grad_squeeze, "dp", scatter_dimension=0, tiled=True),
        lax.psum_scatter(grad_expand, "dp", scatter_dimension=0, tiled=True),
        lax.psum_scatter(grad_last, "dp", scatter_dimension=0, tiled=True),
    )
    owned = lax.psum(
        (partial_value[0], partial_value[1], partial_value[2], partial_value[3], partial_value[4]),
        "rep",
    )
    shard_length = norm_params.shape[0]
    norm_grad_owned = lax.dynamic_slice_in_dim(
        grad_norms, lax.axis_index("dp") * shard_length, shard_length
    )
    reduce_new = adamw(
        reduce_weight, reduce_moment, reduce_second, owned[0], 2.0 * CHANNELS ** (-0.5), DECAY
    )
    conv_new = adamw(
        conv_weight,
        conv_moment,
        conv_second,
        owned[1],
        2.0 * (9 * BOTTLE // RADIX) ** (-0.5),
        DECAY,
    )
    squeeze_new = adamw(
        squeeze_weight, squeeze_moment, squeeze_second, owned[2], 2.0 * BOTTLE ** (-0.5), DECAY
    )
    expand_new = adamw(
        expand_weight, expand_moment, expand_second, owned[3], 2.0 * (INNER // 8) ** (-0.5), DECAY
    )
    project_new = adamw(
        project_weight, project_moment, project_second, owned[4], 2.0 * BOTTLE ** (-0.5), DECAY
    )
    norm_new = adamw(norm_params, norm_moment, norm_second, norm_grad_owned, NORM_RATE, 0.0)
    return (
        jnp.concatenate(outputs, axis=0),
        jnp.concatenate(input_grads, axis=0),
        reduce_new[0],
        reduce_new[1],
        reduce_new[2],
        conv_new[0],
        conv_new[1],
        conv_new[2],
        squeeze_new[0],
        squeeze_new[1],
        squeeze_new[2],
        expand_new[0],
        expand_new[1],
        expand_new[2],
        project_new[0],
        project_new[1],
        project_new[2],
        norm_new[0],
        norm_new[1],
        norm_new[2],
    )


MESH = pl.DeviceIdType.MESH
PAD = 64
CHUNK = 112
F32 = jnp.float32
BF16 = jnp.bfloat16
STATS = {
    "reduced": (8, 128),
    "widened0": (8, 128),
    "widened1": (8, 128),
    "pool": (8, 128),
    "images": (16, 128),
    "projected0": (8, 256),
    "projected1": (8, 256),
    "back_projected0": (8, 256),
    "back_projected1": (8, 256),
    "back_pool": (8, 128),
    "back_widened0": (8, 128),
    "back_widened1": (16, 128),
    "back_reduced0": (8, 128),
    "back_reduced1": (8, 128),
}
DIRECT = ("reduced", "pool", "back_pool")


def sigmoid(values):
    return 0.5 * jnp.tanh(0.5 * values) + 0.5


def row_ids(width):
    return lax.broadcasted_iota(jnp.int32, (8, width), 0)


def image_sum(rows):
    return rows + pltpu.roll(rows, 4, 0)


def pair_sum(rows):
    even = row_ids(rows.shape[1]) % 2 == 0
    return rows + jnp.where(even, pltpu.roll(rows, 7, 0), pltpu.roll(rows, 1, 0))


def micro_sum(rows):
    return pair_sum(image_sum(rows))


def stack_sums(first, second):
    return jnp.where(row_ids(first.shape[1]) < 4, first, second)


def unstack_sums(stacked):
    upper = row_ids(stacked.shape[1]) < 4
    turned = pltpu.roll(stacked, 4, 0)
    return jnp.where(upper, stacked, turned), jnp.where(upper, turned, stacked)


def fold_lanes(stacked):
    half = stacked.shape[1] // 2
    even = row_ids(half) % 2 == 0
    return jnp.where(even, stacked[:, :half], stacked[:, half:])


def unfold_lanes(folded):
    even = row_ids(folded.shape[1]) % 2 == 0
    left = jnp.where(even, folded, pltpu.roll(folded, 1, 0))
    right = jnp.where(even, pltpu.roll(folded, 7, 0), folded)
    return jnp.concatenate([left, right], axis=1)


def norm_terms(total, square, gain, bias, count):
    center = total * (1.0 / count)
    scale = lax.rsqrt(square * (1.0 / count) - center * center + EPSILON)
    slope = scale * gain
    return center, scale, slope, bias - center * slope


def back_terms(center, scale, slope, bias_sum, gain_sum, count):
    by_value = -slope * scale * (gain_sum * (1.0 / count))
    constant = -slope * (bias_sum * (1.0 / count)) - by_value * center
    return by_value, constant


def tdot(left, right):
    return lax.dot_general(left, right, (((0,), (0,)), ((), ())), preferred_element_type=F32)


def dot_t(left, right):
    return lax.dot_general(left, right, (((1,), (1,)), ((), ())), preferred_element_type=F32)


def in_parts(values, parts):
    found = []
    for _ in range(parts):
        rounded = values.astype(BF16).astype(F32)
        found.append(rounded)
        values = values - rounded
    return found


def exact_dot(left, right, transposed):
    stacked = jnp.concatenate(in_parts(left, 3), axis=0).astype(BF16)
    wide = dot_t(stacked, right) if transposed else jnp.dot(stacked, right, preferred_element_type=F32)
    return wide[0:8] + wide[8:16] + wide[16:24]


def row_dot(left, right):
    high, low = in_parts(left, 2)
    other_high, other_low = in_parts(right, 2)
    return tdot(
        jnp.concatenate([high, high, low, low], axis=0).astype(BF16),
        jnp.concatenate([other_high, other_low, other_high, other_low], axis=0).astype(BF16),
    )


def image_dot(left, right):
    return row_dot(jnp.where(row_ids(left.shape[1]) < 4, left, 0.0), right)


def block_kernel(
    n_dp,
    n_rep,
    x_hbm,
    gy_hbm,
    w1_hbm,
    wc_hbm,
    sq_hbm,
    ex_hbm,
    w3_hbm,
    np_hbm,
    bo_hbm,
    dx_hbm,
    f1_hbm,
    fc_hbm,
    f3_hbm,
    fe_hbm,
    gn_hbm,
    w1_own,
    wc_own,
    sq_own,
    ex_own,
    w3_own,
    np_own,
    gn_out,
    x4,
    gy4,
    x_v,
    gy_v,
    fw1,
    fwc,
    fes,
    fw3,
    es_own,
    np_slots,
    np_full,
    red,
    act,
    columns,
    wid,
    splits,
    mixed,
    proj,
    up,
    bo4,
    dx4,
    dproj,
    d_mixed,
    dn2,
    dwid,
    dcol,
    dn1,
    dred,
    g1,
    gc,
    g3,
    ge,
    gb,
    fix,
    back_own,
    *rest,
):
    n_ar = len(STATS)
    order = {name: k for k, name in enumerate(STATS)}
    ar_slots_a = dict(zip(STATS, rest[0:n_ar]))
    ar_slots_b = dict(zip(STATS, rest[n_ar : 2 * n_ar]))
    rest = rest[2 * n_ar :]
    r1s, ys, r2s, ks, r3s, own = (rest[6 * i : 6 * i + 6] for i in range(6))
    fs = rest[36:40]
    rest = rest[40:]
    local_sem, ar_send_a, ar_recv_a, ar_send_b, ar_recv_b, np_sems, ws, wr, gs, gr = rest

    dp = lax.axis_index("dp")
    rep = lax.axis_index("rep")
    core = lax.rem(rep, 2)
    half_y = lax.div(rep, 2)
    planes = n_dp // 2
    plane_size = 2 * n_rep
    plane = lax.div(dp, 2)
    in_plane = lax.rem(dp, 2) * n_rep + rep
    sibling = (dp, half_y * 2 + (1 - core))
    across = (dp, (1 - half_y) * 2 + core)
    pixels = float(SIDE * SIDE * 2 * n_dp * n_rep)
    pictures = float(2 * n_dp * n_rep)

    x = lax.rem(dp, 2)
    if planes == 4:
        upper = lax.div(plane, 2)
        other_planes = [3 - 3 * upper, 2 - upper, 1 - plane + 4 * upper]
    else:
        other_planes = [lax.rem(plane + step, planes) for step in range(1, planes)]
    flips = ((1, 1, 1), (1, 1, 0), (1, 0, 1), (1, 0, 0), (0, 1, 1), (0, 1, 0), (0, 0, 1), (0, 0, 0))

    def of_flip(z, flip):
        there = [1 - own if turn else own for own, turn in zip((x, half_y, core), flip)]
        return (z * 2 + there[0], there[1] * 2 + there[2])

    plane_peers = [of_flip(plane, flip) for flip in flips[:-1]]
    column_peers = [of_flip(z, flips[-1]) for z in other_planes]
    owner_peers = [of_flip(z, flip) for z in other_planes for flip in (flips[3], flips[7])]
    owner_peers += [of_flip(plane, flips[3])]
    all_peers = [of_flip(z, flip) for z in other_planes for flip in flips] + plane_peers
    me, everyone = dp * n_rep + rep, n_dp * n_rep
    rep_peers = [(dp, lax.rem(rep + step, n_rep)) for step in range(1, n_rep)]

    def remote(src, dst, send_sem, recv_sem, device):
        return pltpu.make_async_remote_copy(
            src_ref=src,
            dst_ref=dst,
            send_sem=send_sem,
            recv_sem=recv_sem,
            device_id=device,
            device_id_type=MESH,
        )

    def send_all(ref, send_sem, recv_sem, peers):
        for device in peers:
            remote(ref, ref, send_sem, recv_sem, device).start()

    def wait_bytes(ref, sem):
        pltpu.make_async_copy(ref, ref, sem).wait()

    def over_rows(body, init):
        def step(index, carry):
            return body(pl.multiple_of(index * CHUNK, CHUNK), carry)

        return lax.fori_loop(0, ROWS // CHUNK, step, init)

    def grouped(values):
        return values.reshape(CHUNK // 8, 8, values.shape[-1])

    def by_four(values):
        return flat(values).reshape(CHUNK // 4, 4, values.shape[-1])

    def flat(values):
        return values.reshape(CHUNK, values.shape[-1])

    own_copies = [
        pltpu.make_async_copy(source, target, local_sem.at[4 + k])
        for k, (source, target) in enumerate(
            (
                (w1_hbm, w1_own),
                (np_hbm, np_own),
                (wc_hbm, wc_own),
                (w3_hbm, w3_own),
                (sq_hbm, sq_own),
                (ex_hbm, ex_own),
            )
        )
    ]
    for copy in own_copies:
        copy.start()
    x_copy = pltpu.make_async_copy(x_hbm, x4, local_sem.at[0])
    gy_copy = pltpu.make_async_copy(gy_hbm, gy4, local_sem.at[1])
    x_copy.start()
    barrier = pltpu.get_barrier_semaphore()
    for device in all_peers:
        pl.semaphore_signal(barrier, inc=1, device_id=device, device_id_type=MESH)

    part = core * 2 + half_y
    own_copies[0].wait()
    q1 = w1_own.shape[0] // 4
    fw1[dp, core, half_y] = w1_own[pl.ds(pl.multiple_of(part * q1, q1), q1), :].astype(BF16)
    core_lanes = pl.ds(pl.multiple_of(core * 128, 128), 128)
    es_lanes = pl.ds(pl.multiple_of(part * 128, 128), 128)
    w3_lanes = pl.ds(pl.multiple_of(part * 256, 128), 256)

    pl.semaphore_wait(barrier, everyone - 1)

    def quarter_w1(c, y):
        return fw1.at[:, c, y]

    def quarter_wc(c, y):
        return fwc.at[:, y, :, pl.ds(pl.multiple_of(c * 128, 128), 128)]

    def quarter_es(c, y):
        return fes.at[:, :, pl.ds(pl.multiple_of((c * 2 + y) * 128, 128), 128)]

    def quarter_w3(c, y):
        return fw3.at[:, :, pl.ds(pl.multiple_of((c * 2 + y) * 256, 128), 256)]

    quarters = (quarter_w1, quarter_wc, quarter_es, quarter_w3)

    def piece(which, d):
        return (
            fw1.at[d, core, half_y],
            fwc.at[d, half_y, :, core_lanes],
            fes.at[d, :, es_lanes],
            fw3.at[d, :, w3_lanes],
        )[which]

    def seven(which):
        return (
            fw1.at[pl.ds(0, n_dp - 1), core, half_y],
            fwc.at[pl.ds(0, n_dp - 1), half_y, :, core_lanes],
            fes.at[pl.ds(0, n_dp - 1), :, es_lanes],
            fw3.at[pl.ds(0, n_dp - 1), :, w3_lanes],
        )[which]

    def gather_out(which):
        send_all(piece(which, dp), ws.at[which, 0], wr.at[which, 0], owner_peers)

    def gather_turn(which):
        wait_bytes(seven(which), wr.at[which, 0])
        mine = quarters[which](core, half_y)
        remote(mine, mine, ws.at[which, 1], wr.at[which, 1], across).start()
        remote(mine, mine, ws.at[which, 2], wr.at[which, 2], sibling).start()

    def gather_hand(which):
        theirs = quarters[which](core, 1 - half_y)
        wait_bytes(theirs, wr.at[which, 1])
        remote(theirs, theirs, ws.at[which, 3], wr.at[which, 3], sibling).start()

    def gather_end(which):
        wait_bytes(quarters[which](1 - core, half_y), wr.at[which, 2])
        wait_bytes(quarters[which](1 - core, 1 - half_y), wr.at[which, 3])

    def to_rows(source, target):
        def body(index, carry):
            values = source[pl.ds(index * (CHUNK // 4), CHUNK // 4)].astype(F32)
            row = pl.multiple_of(index * CHUNK, CHUNK)
            target[pl.ds(row, CHUNK), :] = values.reshape(CHUNK, CHANNELS).astype(BF16)
            return carry

        lax.fori_loop(0, ROWS // CHUNK, body, 0)

    gather_out(0)
    own_copies[2].wait()
    qc = wc_own.shape[0] // 2
    fwc[dp, half_y, :, core_lanes] = wc_own[
        pl.ds(pl.multiple_of(half_y * qc, qc), qc), core_lanes
    ].astype(BF16)
    gather_out(1)

    own_copies[1].wait()
    shard = np_own.shape[0]
    lanes_id = lax.broadcasted_iota(jnp.int32, (8, 128), 1)
    turn = lax.rem(shard * dp, 128)
    np_rows = []
    for at in range(0, shard, 128):
        width = min(128, shard - at)
        piece_row = np_own[pl.ds(at, width)].reshape(1, width)
        if width < 128:
            piece_row = jnp.concatenate([piece_row, jnp.zeros((1, 128 - width), F32)], axis=1)
        np_rows.append(piece_row)
    np_rows.append(jnp.zeros((8 - len(np_rows), 128), F32))
    np_turned = jnp.concatenate(np_rows, axis=0).astype(BF16).astype(F32)
    np_turned = pltpu.roll(np_turned, turn, 1)
    np_slots[dp] = jnp.where(lanes_id < turn, pltpu.roll(np_turned, 1, 0), np_turned)
    send_all(np_slots.at[dp], np_sems.at[0], np_sems.at[1], owner_peers)
    for copy in own_copies[3:]:
        copy.wait()
    ex_rows = ex_own.shape[0]
    es_own[:, 0:128] = sq_own[...].astype(BF16)
    es_own[0:ex_rows, 128:384] = ex_own[:, 0:256].astype(BF16)
    es_own[ex_rows : 2 * ex_rows, 128:384] = ex_own[:, 256:512].astype(BF16)
    es_own[:, 384:512] = jnp.zeros((2 * ex_rows, 128), BF16)
    fes[dp, :, es_lanes] = es_own[:, es_lanes]
    fw3[dp, :, w3_lanes] = w3_own[:, w3_lanes].astype(BF16)
    gy_copy.start()
    x_copy.wait()
    to_rows(x4, x_v)
    gather_turn(0)
    zero_rows = jnp.zeros((PAD, BOTTLE), F32)
    for side in range(3):
        act[side, 0:PAD, :] = zero_rows
        act[side, PAD + ROWS : 2 * PAD + ROWS, :] = zero_rows
    for lane_block in range(9):
        dcol[0:PAD, lane_block * 256 : lane_block * 256 + 256] = zero_rows
        dcol[PAD + ROWS : 2 * PAD + ROWS, lane_block * 256 : lane_block * 256 + 256] = zero_rows
    gather_hand(0)
    gather_out(2)
    gather_out(3)
    gather_turn(1)

    def sum_start(k, payload):
        if k in DIRECT:
            ar_slots_a[k][me] = payload
            send_all(ar_slots_a[k].at[me], ar_send_a.at[order[k]], ar_recv_a.at[order[k]], all_peers)
        else:
            ar_slots_a[k][in_plane] = payload
            send_all(ar_slots_a[k].at[in_plane], ar_send_a.at[order[k]], ar_recv_a.at[order[k]], plane_peers)

    def sum_slots(slots, count):
        sums = [slots[slot] for slot in range(count)]
        while len(sums) > 1:
            sums = [sums[i] + sums[i + 1] for i in range(0, len(sums), 2)]
        return sums[0]

    def sum_turn(k):
        if k in DIRECT:
            return
        wait_bytes(ar_slots_a[k].at[pl.ds(0, plane_size - 1)], ar_recv_a.at[order[k]])
        ar_slots_b[k][plane] = sum_slots(ar_slots_a[k], plane_size)
        send_all(ar_slots_b[k].at[plane], ar_send_b.at[order[k]], ar_recv_b.at[order[k]], column_peers)

    def sum_end(k):
        if k in DIRECT:
            wait_bytes(ar_slots_a[k].at[pl.ds(0, everyone - 1)], ar_recv_a.at[order[k]])
            return sum_slots(ar_slots_a[k], everyone)
        wait_bytes(ar_slots_b[k].at[pl.ds(0, planes - 1)], ar_recv_b.at[order[k]])
        return sum_slots(ar_slots_b[k], planes)

    def lanes_of(index, width):
        return pl.ds(pl.multiple_of(index * width, 128), width)

    cut = 64
    conv_rows = {1: pl.ds(0, cut), 2: pl.ds(cut, gc.shape[2] - cut)}
    grads = (g1, gc, gc, g3, ge, gb)
    turned_kinds = (0, 5)

    def half_of(which, c):
        ref = grads[which]
        if which in turned_kinds:
            return ref.at[c]
        if which in conv_rows:
            return ref.at[:, :, conv_rows[which], lanes_of(c, 128)]
        return ref.at[:, :, lanes_of(c, (512, 256)[which - 3])]

    def y_part(which, ref, y):
        if which in turned_kinds:
            return ref.at[y]
        if which < 3:
            return ref.at[:, y]
        return ref.at[:, :, lanes_of(y, (256, 128)[which - 3])]

    def quarter_of(which, c, y):
        ref = grads[which]
        if which in turned_kinds:
            return ref.at[c, y]
        if which in conv_rows:
            return ref.at[:, y, conv_rows[which], lanes_of(c, 128)]
        return ref.at[:, :, lanes_of(c * 2 + y, (256, 128)[which - 3])]

    def final_part(which, c, y):
        if which == 0:
            return fs[0].at[c, y]
        if which in conv_rows:
            return fs[1].at[y, conv_rows[which], lanes_of(c, 128)]
        return fs[which - 1].at[:, lanes_of(c * 2 + y, (256, 128)[which - 3])]

    def of_owner(which, ref, d):
        return ref.at[:, lanes_of(d, CHANNELS // n_dp)] if which in turned_kinds else ref.at[d]

    def in_blocks(which, body):
        if which in turned_kinds:
            count = 4
            rows = grads[which].shape[2] // count
            block = lambda index: pl.ds(pl.multiple_of(index * rows, rows), rows)
        else:
            count, block = n_dp, lambda index: index

        def step(index, carry):
            body(block(index))
            return carry

        lax.fori_loop(0, count, step, 0)

    def reduce_core(which):
        remote(
            half_of(which, 1 - core), r1s[which], gs.at[which, 0], gr.at[which, 0], sibling
        ).start()

    def reduce_y(which):
        wait_bytes(r1s[which], gr.at[which, 0])
        away = quarter_of(which, core, 1 - half_y)
        mine = quarter_of(which, core, half_y)
        there = y_part(which, r1s[which], 1 - half_y)
        here = y_part(which, r1s[which], half_y)

        def add_away(at):
            ys[which][at] = (away[at].astype(F32) + there[at].astype(F32)).astype(
                ys[which].dtype
            )

        in_blocks(which, add_away)
        remote(ys[which], r2s[which], gs.at[which, 1], gr.at[which, 1], across).start()

        def add_mine(at):
            mine[at] = (mine[at].astype(F32) + here[at].astype(F32)).astype(mine.dtype)

        in_blocks(which, add_mine)

    def reduce_owner(which):
        wait_bytes(r2s[which], gr.at[which, 1])
        mine = quarter_of(which, core, half_y)

        def add(at):
            ks[which][at] = (mine[at].astype(F32) + r2s[which][at].astype(F32)).astype(
                ks[which].dtype
            )

        in_blocks(which, add)
        for device in owner_peers:
            remote(
                of_owner(which, ks[which], device[0]),
                r3s[which].at[dp],
                gs.at[which, 2],
                gr.at[which, 2],
                device,
            ).start()
        own[which][...] = of_owner(which, mine, dp)[...].astype(F32) + of_owner(
            which, r2s[which], dp
        )[...].astype(F32)
        r3s[which][dp] = jnp.zeros(own[which].shape, r3s[which].dtype)

    def owner_total(which):
        wait_bytes(r3s[which].at[pl.ds(0, n_dp - 1)], gr.at[which, 2])
        total = own[which][...]
        for slot in range(n_dp):
            total = total + r3s[which][slot].astype(F32)
        return total

    def reduce_spread(which):
        total = owner_total(which)
        if which == 0:
            rows = pl.ds(pl.multiple_of(part * (BOTTLE // 4), BOTTLE // 4), BOTTLE // 4)
            total = total - fix[0, rows, :]
            for m in range(2):
                total = total - fix[1 + m, rows, :] * back_own[m]
        mine = final_part(which, core, half_y)
        mine[...] = total
        send_all(mine, gs.at[which, 3], gr.at[which, 3], rep_peers)

    def three_parts(which):
        if which == 0:
            return r1s[0].at[0, :, pl.ds(0, 3 * CHANNELS // n_dp)]
        return r1s[which].at[pl.ds(0, 3), 0] if which < 3 else y_part(which, r1s[which], 0).at[pl.ds(0, 3)]

    def reduce_end(which):
        wait_bytes(three_parts(which), gr.at[which, 3])

    gather_end(0)
    red[...] = jnp.dot(x_v[...], fw1[...].reshape(CHANNELS, BOTTLE), preferred_element_type=F32)

    def sums_of(ref, start, width):
        def body(row, carry):
            values = grouped(ref[pl.ds(row, CHUNK), start : start + width])
            return carry[0] + jnp.sum(values, axis=0), carry[1] + jnp.sum(values * values, axis=0)

        zero = jnp.zeros((8, width), F32)
        return over_rows(body, (zero, zero))

    def joined(found):
        both = [jnp.concatenate(item, axis=1) for item in zip(*found)]
        return fold_lanes(stack_sums(micro_sum(both[0]), micro_sum(both[1])))

    def both_sums(name):
        return unstack_sums(unfold_lanes(sum_end(name)))

    sum_start("reduced", joined([sums_of(red, 0, 256)]))
    gather_turn(2)

    gy_copy.wait()
    to_rows(gy4, gy_v)
    wait_bytes(np_slots.at[pl.ds(0, n_dp - 1)], np_sems.at[1])
    np_full[...] = jnp.zeros(np_full.shape, F32)
    for d in range(n_dp):
        at = shard * d // 128
        np_full[at : at + 8, :] = np_full[at : at + 8, :] + np_slots[d]

    def vector(at, width):
        rows = [np_full[at // 128 + k : at // 128 + k + 1, :] for k in range(width // 128)]
        return jnp.concatenate(rows, axis=1) if len(rows) > 1 else rows[0]

    gain_one, bias_one = vector(0, 256), vector(256, 256)
    gain_two, bias_two = vector(512, 512), vector(1024, 512)
    gain_pool, bias_pool = vector(1536, 128), vector(1664, 128)
    bias_expand = vector(1792, 512)
    gain_three, bias_three = vector(2304, 1024), vector(3328, 1024)

    total, square = both_sums("reduced")
    center1, scale1, mul1, add1 = norm_terms(total, square, gain_one, bias_one, pixels)

    def make_active(row, carry):
        turned = grouped(red[pl.ds(row, CHUNK), :]) * mul1 + add1
        act[1, pl.ds(PAD + row, CHUNK), :] = flat(turned * sigmoid(turned))
        return carry

    over_rows(make_active, 0)
    gather_hand(1)
    gather_hand(2)
    gather_turn(3)
    place = lax.rem(lax.broadcasted_iota(jnp.int32, (CHUNK, BOTTLE), 0) // 4, SIDE)
    not_last = place != SIDE - 1
    not_first = place != 0

    def beside(side, row, distance, lanes=slice(0, BOTTLE)):
        near = act[side, pl.ds(PAD + row - 8, CHUNK + 16), lanes]
        return pltpu.roll(near, (CHUNK + 16 - distance) % (CHUNK + 16), 0)[8 : 8 + CHUNK]

    def shift_active(row, carry):
        act[2, pl.ds(PAD + row, CHUNK), :] = jnp.where(not_last, beside(1, row, 4), 0.0)
        act[0, pl.ds(PAD + row, CHUNK), :] = jnp.where(not_first, beside(1, row, -4), 0.0)
        return carry

    over_rows(shift_active, 0)

    def make_columns(row, carry):
        for tap in range(9):
            down, side = tap // 3 - 1, tap % 3
            values = act[side, pl.ds(PAD + row + 56 * down, CHUNK), :].astype(BF16)
            columns[0, pl.ds(row, CHUNK), tap * 128 : tap * 128 + 128] = values[:, 0:128]
            columns[1, pl.ds(row, CHUNK), tap * 128 : tap * 128 + 128] = values[:, 128:256]
        return carry

    over_rows(make_columns, 0)
    gather_end(1)
    own_half = n_dp // 2

    def filters(group):
        return fwc[group * own_half : (group + 1) * own_half].reshape(9 * 128, BOTTLE)

    halves2 = (slice(0, 256), slice(256, 512))
    for group, lanes in enumerate(halves2):
        wid[:, lanes] = jnp.dot(columns[group], filters(group), preferred_element_type=F32)
        sum_start(f"widened{group}", joined([sums_of(wid, group * 256, 256)]))
    sum_turn("widened0")
    sum_turn("widened1")
    gather_hand(3)

    norm2 = []
    pooled = jnp.zeros((8, BOTTLE), F32)
    for group, lanes in enumerate(halves2):
        total, square = both_sums(f"widened{group}")
        norm2.append(norm_terms(total, square, gain_two[:, lanes], bias_two[:, lanes], pixels))
        m2, a2 = norm2[group][2:4]

        def make_splits(row, carry):
            turned = grouped(wid[pl.ds(row, CHUNK), lanes]) * m2 + a2
            values = turned * sigmoid(turned)
            splits[pl.ds(row, CHUNK), lanes] = flat(values)
            return carry + jnp.sum(values, axis=0)

        pooled = over_rows(make_splits, pooled)
    pooled = image_sum(pooled) * (1.0 / (SIDE * SIDE))
    gather_end(2)
    squeeze = fes[:, :, 0:128].reshape(BOTTLE, INNER)
    ex_both = fes[:, :, 128:384]
    expand = jnp.concatenate(
        [
            ex_both[:, 0:ex_rows].reshape(INNER, 256),
            ex_both[:, ex_rows : 2 * ex_rows].reshape(INNER, 256),
        ],
        axis=1,
    )
    pre_pool = exact_dot(pooled, squeeze, False)
    sum_start("pool", stack_sums(pair_sum(pre_pool), pair_sum(pre_pool * pre_pool)))
    first_micro = lax.rem(row_ids(BOTTLE), 4) < 2

    def make_normed(row, carry):
        rows = pl.ds(row, CHUNK)
        normed = (grouped(red[rows, :]) - center1) * scale1
        dwid[rows, 0:256] = flat(jnp.where(first_micro, normed, 0.0)).astype(BF16)
        dwid[rows, 256:512] = flat(jnp.where(first_micro, 0.0, normed)).astype(BF16)
        return carry + jnp.sum(grouped(x_v[rows, :].astype(F32)), axis=0)

    image_sums = micro_sum(over_rows(make_normed, jnp.zeros((8, CHANNELS), F32)))
    sum_start(
        "images",
        jnp.concatenate(
            [
                image_sums[2 * m : 2 * m + 1, at : at + 128]
                for m in range(2)
                for at in range(0, CHANNELS, 128)
            ],
            axis=0,
        ),
    )
    normed_images = tdot(dwid[...], x_v[...]).astype(BF16)
    normed_images = normed_images.reshape(2, 2, 2, BOTTLE // 4, CHANNELS)
    for m in range(2):
        gb[:, :, m * (BOTTLE // 4) : (m + 1) * (BOTTLE // 4)] = normed_images[m]
    reduce_core(5)
    total, square = unstack_sums(sum_end("pool"))
    center_p, scale_p, mul_p, add_p = norm_terms(total, square, gain_pool, bias_pool, pictures)
    normed_p = (pre_pool - center_p) * scale_p
    norm_p = pre_pool * mul_p + add_p
    gate_p = sigmoid(norm_p)
    hidden = norm_p * gate_p
    slope_p = gate_p * (1.0 + norm_p * (1.0 - gate_p))
    logits = exact_dot(hidden, expand, False) + bias_expand
    left, right = logits[:, 0:256], logits[:, 256:512]
    most = jnp.maximum(left, right)
    left, right = jnp.exp(left - most), jnp.exp(right - most)
    att0 = left / (left + right)
    att1 = right / (left + right)

    gather_end(3)
    last = fw3[...].reshape(BOTTLE, CHANNELS)
    def make_mixed(row, carry):
        rows = pl.ds(row, CHUNK)
        values = grouped(splits[rows, 0:256]) * att0 + grouped(splits[rows, 256:512]) * att1
        mixed[rows, :] = flat(values).astype(BF16)
        return carry

    over_rows(make_mixed, 0)
    halves3 = (slice(0, 512), slice(512, 1024))
    blocks3 = [[slice(512 * h + k, 512 * h + k + 256) for k in (0, 256)] for h in range(2)]
    for half, lanes in enumerate(halves3):
        proj[:, lanes] = jnp.dot(mixed[...], last[:, lanes], preferred_element_type=F32)
        sum_start(
            f"projected{half}", joined([sums_of(proj, 512 * half + k, 256) for k in (0, 256)])
        )
    sum_turn("projected0")
    sum_turn("projected1")
    sum_turn("images")
    reduce_y(5)

    norm3 = []
    zero = jnp.zeros((8, 256), F32)
    for half, lanes in enumerate(halves3):
        total, square = both_sums(f"projected{half}")
        norm3.append(norm_terms(total, square, gain_three[:, lanes], bias_three[:, lanes], pixels))
        found = []
        for k, block in enumerate(blocks3[half]):
            c3, s3, m3, a3 = (item[:, k * 256 : k * 256 + 256] for item in norm3[half])

            def make_out(row, carry):
                rows = pl.ds(row, CHUNK)
                values = grouped(proj[rows, block])
                summed = grouped(x_v[rows, block].astype(F32)) + (values * m3 + a3)
                gate = sigmoid(summed)
                bo4[pl.ds(row // 4, CHUNK // 4), :, block] = by_four(summed * gate).astype(BF16)
                upstream = grouped(gy_v[rows, block].astype(F32)) * (
                    gate * (1.0 + summed * (1.0 - gate))
                )
                up[rows, block] = flat(upstream)
                normed = (values - c3) * s3
                return carry[0] + jnp.sum(upstream, axis=0), carry[1] + jnp.sum(
                    upstream * normed, axis=0
                )

            found.append(over_rows(make_out, (zero, zero)))
        sum_start(f"back_projected{half}", joined(found))
    bo_copy = pltpu.make_async_copy(bo4, bo_hbm, local_sem.at[2])
    bo_copy.start()

    def write_norm(at, pattern):
        at = at // 128
        both = pattern[0:1, :] + pattern[2:3, :]
        for k in range(both.shape[1] // 128):
            np_full[at + k : at + k + 1, :] = both[:, k * 128 : k * 128 + 128]

    sum_turn("back_projected0")
    sum_turn("back_projected1")
    reduce_owner(5)

    for half, lanes in enumerate(halves3):
        bias_sum, gain_sum = both_sums(f"back_projected{half}")
        write_norm(2304 + 512 * half, gain_sum)
        write_norm(3328 + 512 * half, bias_sum)
        by_value, constant = back_terms(*norm3[half][0:3], bias_sum, gain_sum, pixels)
        for k, block in enumerate(blocks3[half]):
            m3, v3, k3 = (
                item[:, k * 256 : k * 256 + 256] for item in (norm3[half][2], by_value, constant)
            )

            def make_dproj(row, carry):
                rows = pl.ds(row, CHUNK)
                values = grouped(up[rows, block]) * m3 + grouped(proj[rows, block]) * v3 + k3
                dproj[rows, block] = flat(values).astype(BF16)
                return carry

            over_rows(make_dproj, 0)
        part_mixed = dot_t(dproj[:, lanes], last[:, lanes])
        d_mixed[...] = part_mixed if half == 0 else d_mixed[...] + part_mixed

    def attend(row, carry):
        rows = pl.ds(row, CHUNK)
        values = grouped(d_mixed[rows, :])
        return (
            carry[0] + jnp.sum(values * grouped(splits[rows, 0:256]), axis=0),
            carry[1] + jnp.sum(values * grouped(splits[rows, 256:512]), axis=0),
        )

    d_att0, d_att1 = over_rows(attend, (zero, zero))
    d_att0, d_att1 = image_sum(d_att0), image_sum(d_att1)
    both = att0 * d_att0 + att1 * d_att1
    d_logits = jnp.concatenate([att0 * (d_att0 - both), att1 * (d_att1 - both)], axis=1)
    d_hidden = exact_dot(d_logits, expand, True)
    d_pool = d_hidden * slope_p
    per_micro = stack_sums(pair_sum(d_pool), pair_sum(d_pool * normed_p))
    sum_start("back_pool", per_micro)
    ex_sum = pair_sum(d_logits)
    ex_sum = ex_sum + pltpu.roll(ex_sum, 2, 0)
    ex_rows_sum = ex_sum[:, 0:128]
    for k in range(1, 4):
        ex_rows_sum = jnp.where(row_ids(128) == k, ex_sum[:, k * 128 : k * 128 + 128], ex_rows_sum)

    grad_ex = image_dot(hidden, d_logits)
    grad_ex = grad_ex.reshape(n_dp, ex_rows, 512)
    ge[:, 0:ex_rows, 128:384] = grad_ex[:, :, 0:256]
    ge[:, ex_rows : 2 * ex_rows, 128:384] = grad_ex[:, :, 256:512]
    ge[:, :, 384:512] = jnp.zeros((n_dp, 2 * ex_rows, 128), F32)
    g3[...] = tdot(mixed[...], dproj[...]).reshape(g3.shape)
    reduce_core(3)
    held = []
    for group, att in ((0, att0), (1, att1)):
        lanes = halves2[group]
        c2, s2, m2, a2 = norm2[group]

        def make_dn2(row, carry):
            rows = pl.ds(row, CHUNK)
            values = grouped(wid[rows, lanes])
            turned = values * m2 + a2
            gate = sigmoid(turned)
            slope = gate * (1.0 + turned * (1.0 - gate))
            down = grouped(d_mixed[rows, :]) * att * slope
            dn2[rows, lanes] = flat(down)
            splits[rows, lanes] = flat(slope)
            normed = (values - c2) * s2
            terms = (down, down * normed, slope, slope * normed)
            return tuple(item + jnp.sum(term, axis=0) for item, term in zip(carry, terms))

        held.append([image_sum(item) for item in over_rows(make_dn2, (zero,) * 4)])
    pool_bias_sum, pool_gain_sum = unstack_sums(sum_end("back_pool"))
    write_norm(1536, pool_gain_sum)
    write_norm(1664, pool_bias_sum)
    d_pre_pool = mul_p * (
        d_pool - pool_bias_sum * (1.0 / pictures) - normed_p * (pool_gain_sum * (1.0 / pictures))
    )
    d_pooled = exact_dot(d_pre_pool, squeeze, True) * (1.0 / (SIDE * SIDE))
    for group in range(2):
        down, down_normed, slope, slope_normed = held[group]
        payload = fold_lanes(
            stack_sums(
                pair_sum(down + d_pooled * slope), pair_sum(down_normed + d_pooled * slope_normed)
            )
        )
        if group == 1:
            payload = jnp.concatenate([payload, ex_rows_sum], axis=0)
        sum_start(f"back_widened{group}", payload)
    ge[:, :, 0:128] = image_dot(pooled, d_pre_pool).reshape(n_dp, 2 * ex_rows, 128)
    reduce_core(4)
    sum_turn("back_widened0")
    sum_turn("back_widened1")
    reduce_y(3)
    reduce_y(4)
    back_total = owner_total(5)
    back_own[0] = back_total[0 : BOTTLE // 4]
    back_own[1] = back_total[BOTTLE // 4 :]

    small_zero = jnp.zeros((8, 128), F32)
    for group, lanes in enumerate(halves2):
        whole = sum_end(f"back_widened{group}")
        if group == 1:
            np_full[14:18, :] = whole[8:12]
        bias_sum, gain_sum = unstack_sums(unfold_lanes(whole[0:8]))
        write_norm(512 + 256 * group, gain_sum)
        write_norm(1024 + 256 * group, bias_sum)
        m2 = norm2[group][2]
        v2, k2 = back_terms(*norm2[group][0:3], bias_sum, gain_sum, pixels)
        pooled_m2 = d_pooled * m2

        def make_dwid(row, carry):
            rows = pl.ds(row, CHUNK)
            values = grouped(dn2[rows, lanes]) * m2 + grouped(splits[rows, lanes]) * pooled_m2
            values = values + grouped(wid[rows, lanes]) * v2 + k2
            dwid[rows, lanes] = flat(values).astype(BF16)
            return carry

        over_rows(make_dwid, 0)
        gc[group * own_half : (group + 1) * own_half] = tdot(
            columns[group], dwid[:, lanes]
        ).reshape(own_half, 2, 9 * 128 // own_half // 2, BOTTLE)
    reduce_core(1)
    reduce_core(2)
    for group, lanes in enumerate(halves2):
        dcol[PAD : PAD + ROWS, group * 1152 : group * 1152 + 1152] = dot_t(
            dwid[:, lanes], filters(group)
        )
        inner = slice(group * 128, group * 128 + 128)

        def gather_taps(row, carry):
            for side in range(3):
                total = None
                for down in range(3):
                    at = group * 1152 + (3 * down + side) * 128
                    values = dcol[pl.ds(PAD + row - 56 * (down - 1), CHUNK), at : at + 128]
                    total = values if total is None else total + values
                act[side, pl.ds(PAD + row, CHUNK), inner] = total
            return carry

        over_rows(gather_taps, 0)
        c1, s1, m1, a1 = (item[:, inner] for item in (center1, scale1, mul1, add1))
        not_first1, not_last1 = not_first[:, inner], not_last[:, inner]

        def make_dn1(row, carry):
            rows = pl.ds(row, CHUNK)
            d_active = act[1, pl.ds(PAD + row, CHUNK), inner]
            d_active = d_active + jnp.where(not_first1, beside(2, row, -4, inner), 0.0)
            d_active = d_active + jnp.where(not_last1, beside(0, row, 4, inner), 0.0)
            values = grouped(red[rows, inner])
            turned = values * m1 + a1
            gate = sigmoid(turned)
            slope = gate * (1.0 + turned * (1.0 - gate))
            down = grouped(d_active) * slope
            dn1[rows, inner] = flat(down)
            mixed[rows, inner] = flat(down * m1).astype(BF16)
            normed = (values - c1) * s1
            return carry[0] + jnp.sum(down, axis=0), carry[1] + jnp.sum(down * normed, axis=0)

        bias_sum, gain_sum = over_rows(make_dn1, (small_zero, small_zero))
        sum_start(f"back_reduced{group}", stack_sums(micro_sum(bias_sum), micro_sum(gain_sum)))
        if group == 0:
            reduce_owner(3)
            reduce_owner(4)
            reduce_y(1)
    reduce_y(2)
    sum_turn("back_reduced0")
    sum_turn("back_reduced1")
    g1[...] = tdot(mixed[...], x_v[...]).reshape(g1.shape)
    reduce_core(0)
    found = [unstack_sums(sum_end(f"back_reduced{group}")) for group in range(2)]
    bias_sum, gain_sum = (jnp.concatenate(item, axis=1) for item in zip(*found))
    write_norm(0, gain_sum)
    write_norm(256, bias_sum)
    by_value, constant = back_terms(center1, scale1, mul1, bias_sum, gain_sum, pixels)
    def make_dred(row, carry):
        rows = pl.ds(row, CHUNK)
        values = grouped(dn1[rows, :]) * mul1 + grouped(red[rows, :]) * by_value + constant
        dred[rows, :] = flat(values).astype(BF16)
        return carry

    over_rows(make_dred, 0)
    reduce_owner(1)
    proj[...] = dot_t(dred[...], fw1[...].reshape(CHANNELS, BOTTLE))
    reduce_y(0)

    by_bias = mul1 * bias_sum * (1.0 / pixels)
    by_gain = mul1 * gain_sum * (1.0 / pixels)
    image_sums = sum_end("images")
    ids = lax.broadcasted_iota(jnp.int32, (16, 128), 0)
    own_sums = [
        jnp.sum(jnp.where(ids == m * n_dp + dp, image_sums, 0.0), axis=0, keepdims=True)
        for m in range(2)
    ]
    ids = row_ids(128)
    fix[0] = row_dot(by_bias, jnp.where(ids == 0, own_sums[0], jnp.where(ids == 2, own_sums[1], 0.0)))
    for m in range(2):
        fix[1 + m] = row_dot(by_gain, jnp.where(ids == 2 * m, 1.0, 0.0))
    reduce_spread(3)
    reduce_spread(4)

    def make_dx(row, carry):
        for start in range(0, CHANNELS, 256):
            lanes = slice(start, start + 256)
            values = up[pl.ds(row, CHUNK), lanes] + proj[pl.ds(row, CHUNK), lanes]
            dx4[pl.ds(row // 4, CHUNK // 4), :, lanes] = values.reshape(CHUNK // 4, 4, 256)
        return carry

    over_rows(make_dx, 0)
    dx_copy = pltpu.make_async_copy(dx4, dx_hbm, local_sem.at[3])
    dx_copy.start()
    norm_rows = np_full[0:8, :]
    for d in range(1, n_dp):
        at = shard * d // 128
        norm_rows = jnp.where(dp == d, np_full[at : at + 8, :], norm_rows)
    norm_rows = pltpu.roll(norm_rows, lax.rem(128 - turn, 128), 1)
    gn_out[...] = jnp.where(lanes_id < 128 - turn, norm_rows, pltpu.roll(norm_rows, 7, 0))
    reduce_owner(2)
    reduce_owner(0)
    reduce_spread(1)
    reduce_spread(2)
    reduce_spread(0)
    out_copies = [
        pltpu.make_async_copy(source, target, local_sem.at[10 + k])
        for k, (source, target) in enumerate(
            (
                (gn_out, gn_hbm),
                (fs[2], f3_hbm),
                (fs[3], fe_hbm),
                (fs[1], fc_hbm),
                (fs[0], f1_hbm),
            )
        )
    ]
    out_copies[0].start()
    for which in (3, 4, 1, 2, 0):
        reduce_end(which)
        if which != 1:
            out_copies[{3: 1, 4: 2, 2: 3, 0: 4}[which]].start()

    bo_copy.wait()
    dx_copy.wait()
    for copy in out_copies:
        copy.wait()
    for k in STATS:
        if k in DIRECT:
            wait_bytes(ar_slots_a[k].at[pl.ds(0, everyone - 1)], ar_send_a.at[order[k]])
        else:
            wait_bytes(ar_slots_a[k].at[pl.ds(0, plane_size - 1)], ar_send_a.at[order[k]])
            wait_bytes(ar_slots_b[k].at[pl.ds(0, planes - 1)], ar_send_b.at[order[k]])
    wait_bytes(np_slots.at[pl.ds(0, n_dp - 1)], np_sems.at[0])
    for which in range(4):
        wait_bytes(seven(which), ws.at[which, 0])
        for stage in range(1, 4):
            wait_bytes(quarters[which](core, half_y), ws.at[which, stage])
    for which in range(6):
        wait_bytes(r1s[which], gs.at[which, 0])
        wait_bytes(r2s[which], gs.at[which, 1])
        wait_bytes(r3s[which].at[pl.ds(0, n_dp - 1)], gs.at[which, 2])
        if which < 5:
            wait_bytes(three_parts(which), gs.at[which, 3])


def update_kernel(*refs):
    sources, targets = refs[0:25], refs[25:45]
    inputs, outs, through = refs[45:68], refs[68:86], refs[86:88]
    pass_sems, in_sems, out_sems = refs[88:91]
    fetching, passing = [], []
    half = SIDE * SIDE // 2
    for number, (which, at, count) in enumerate(((1, 0, half), (1, half, half), (0, 0, 2 * half))):
        rows = pl.ds(at, count)
        fetching.append(
            pltpu.make_async_copy(
                sources[which].at[rows], through[which].at[rows], pass_sems.at[0, number]
            )
        )
        passing.append(
            pltpu.make_async_copy(
                through[which].at[rows], targets[which].at[rows], pass_sems.at[1, number]
            )
        )
    for copy in fetching:
        copy.start()
    coming = [
        pltpu.make_async_copy(source, held, in_sems.at[k])
        for k, (source, held) in enumerate(zip(sources[2:], inputs))
    ]
    for copy in coming:
        copy.start()
    grads, states = inputs[0:5], inputs[5:23]
    going = [
        pltpu.make_async_copy(held, target, out_sems.at[k])
        for k, (held, target) in enumerate(zip(outs, targets[2:]))
    ]
    ex_rows = states[9].shape[0]
    shard = states[15].shape[0]
    fans = (CHANNELS, 9 * BOTTLE // RADIX, BOTTLE, INNER // 8, BOTTLE)
    for copy in coming[0:5]:
        copy.wait()
    found = (
        grads[0][...].T,
        grads[1][...],
        grads[3][:, 0:128],
        jnp.concatenate([grads[3][0:ex_rows, 128:384], grads[3][ex_rows:, 128:384]], axis=1),
        grads[2][...],
    )
    for order, k in enumerate((3, 2, 4, 0, 1)):
        for copy in coming[5 + 3 * k : 8 + 3 * k]:
            copy.wait()
        new = adamw(
            states[3 * k][...],
            states[3 * k + 1][...],
            states[3 * k + 2][...],
            found[k],
            2.0 * fans[k] ** (-0.5),
            DECAY,
        )
        for j in range(3):
            outs[3 * k + j][...] = new[j]
            going[3 * k + j].start()
        if order < 3:
            fetching[order].wait()
            passing[order].start()
    for copy in coming[20:23]:
        copy.wait()
    for at in range(0, shard, 128):
        width = min(128, shard - at)
        lanes = pl.ds(at, width)
        new = adamw(
            *[states[15 + j][lanes].reshape(1, width) for j in range(3)],
            grads[4][at // 128 : at // 128 + 1, 0:width],
            NORM_RATE,
            0.0,
        )
        for j in range(3):
            outs[15 + j][lanes] = new[j].reshape(width)
    for copy in going[15:18]:
        copy.start()
    for copy in passing + going:
        copy.wait()


def fused_device(
    images,
    out_grad,
    reduce_weight,
    reduce_moment,
    reduce_second,
    conv_weight,
    conv_moment,
    conv_second,
    squeeze_weight,
    squeeze_moment,
    squeeze_second,
    expand_weight,
    expand_moment,
    expand_second,
    project_weight,
    project_moment,
    project_second,
    norm_params,
    norm_moment,
    norm_second,
):
    n_dp, n_rep = lax.axis_size("dp"), lax.axis_size("rep")
    by_pixel = lambda values: jnp.transpose(values, (1, 2, 0, 3)).reshape(-1, 4, CHANNELS)
    qc = conv_weight.shape[0] // 2
    q1 = reduce_weight.shape[0] // 4
    pe = squeeze_weight.shape[0]
    vmem = pltpu.VMEM
    pixel_form = (SIDE * SIDE, 4, CHANNELS)
    scratch = [
        *[
            vmem(values.shape, F32)
            for values in (
                reduce_weight,
                conv_weight,
                squeeze_weight,
                expand_weight,
                project_weight,
                norm_params,
            )
        ],
        vmem((8, 128), F32),
        vmem(pixel_form, BF16),
        vmem(pixel_form, BF16),
        vmem((ROWS, CHANNELS), BF16),
        vmem((ROWS, CHANNELS), BF16),
        vmem((n_dp, 2, 2, q1, BOTTLE), BF16),
        vmem((n_dp, 2, qc, BOTTLE), BF16),
        vmem((n_dp, pe, 512), BF16),
        vmem((n_dp, pe, CHANNELS), BF16),
        vmem((pe, 512), BF16),
        vmem((n_dp, 8, 128), F32),
        vmem((40, 128), F32),
        vmem((ROWS, BOTTLE), F32),
        vmem((3, ROWS + 2 * PAD, BOTTLE), F32),
        vmem((2, ROWS, 9 * 128), BF16),
        vmem((ROWS, 512), F32),
        vmem((ROWS, 512), F32),
        vmem((ROWS, BOTTLE), BF16),
        vmem((ROWS, CHANNELS), F32),
        vmem((ROWS, CHANNELS), F32),
        vmem(pixel_form, BF16),
        vmem(pixel_form, F32),
        vmem((ROWS, CHANNELS), BF16),
        vmem((ROWS, BOTTLE), F32),
        vmem((ROWS, 512), F32),
        vmem((ROWS, 512), BF16),
        vmem((ROWS + 2 * PAD, 2 * 9 * 128), F32),
        vmem((ROWS, BOTTLE), F32),
        vmem((ROWS, BOTTLE), BF16),
        vmem((2, 2, BOTTLE // 4, CHANNELS), F32),
        vmem((n_dp, 2, qc, BOTTLE), F32),
        vmem((n_dp, pe, CHANNELS), F32),
        vmem((n_dp, pe, 512), F32),
        vmem((2, 2, BOTTLE // 2, CHANNELS), BF16),
        vmem((3, BOTTLE, CHANNELS // n_dp), F32),
        vmem((2, BOTTLE // 4, CHANNELS // n_dp), F32),
    ]
    direct = n_dp * n_rep
    scratch += [
        vmem((direct if k in DIRECT else 2 * n_rep,) + shape, F32) for k, shape in STATS.items()
    ]
    scratch += [vmem((n_dp // 2,) + shape, F32) for shape in STATS.values()]
    cut = 64
    lanes1 = CHANNELS // n_dp
    half = [
        (2, BOTTLE // 4, CHANNELS),
        (n_dp, 2, cut, 128),
        (n_dp, 2, qc - cut, 128),
        (n_dp, pe, 512),
        (n_dp, pe, 256),
        (2, BOTTLE // 2, CHANNELS),
    ]
    quarter = [
        (BOTTLE // 4, CHANNELS),
        (n_dp, cut, 128),
        (n_dp, qc - cut, 128),
        (n_dp, pe, 256),
        (n_dp, pe, 128),
        (BOTTLE // 2, CHANNELS),
    ]
    final = [(2, 2, BOTTLE // 4, lanes1), (2, qc, BOTTLE), (pe, CHANNELS), (pe, 512)]
    sent = [BF16, BF16, BF16, BF16, F32, BF16]
    scratch += [vmem(shape, F32) for shape in half[:-1]] + [vmem(half[-1], BF16)]
    scratch += [vmem(shape, kind) for shape, kind in zip(quarter, sent)] * 3
    owned = [(BOTTLE // 4, lanes1)] + [shape[1:] for shape in quarter[1:-1]]
    owned += [(BOTTLE // 2, lanes1)]
    scratch += [vmem((n_dp,) + shape, kind) for shape, kind in zip(owned, sent)]
    scratch += [vmem(shape, F32) for shape in owned]
    scratch += [vmem(shape, F32) for shape in final]
    dma = pltpu.SemaphoreType.DMA
    scratch += [dma((15,))] + [dma((len(STATS),))] * 4 + [dma((2,))] + [dma((4, 4))] * 2 + [dma((6, 4))] * 2
    any_space = pl.BlockSpec(memory_space=pl.ANY)
    block_out, images_grad, sum1, sumc, sum3, sume, norm_grads = pl.pallas_call(
        functools.partial(block_kernel, n_dp, n_rep),
        out_shape=[
            jax.ShapeDtypeStruct(pixel_form, BF16),
            jax.ShapeDtypeStruct(pixel_form, F32),
            *[jax.ShapeDtypeStruct(shape, F32) for shape in final],
            jax.ShapeDtypeStruct((8, 128), F32),
        ],
        in_specs=[any_space] * 8,
        out_specs=[any_space] * 7,
        scratch_shapes=scratch,
        compiler_params=pltpu.CompilerParams(
            collective_id=0, has_side_effects=True, vmem_limit_bytes=63 * 1024 * 1024
        ),
    )(
        by_pixel(images),
        by_pixel(out_grad),
        reduce_weight,
        conv_weight,
        squeeze_weight,
        expand_weight,
        project_weight,
        norm_params,
    )
    states = (
        reduce_weight,
        reduce_moment,
        reduce_second,
        conv_weight,
        conv_moment,
        conv_second,
        squeeze_weight,
        squeeze_moment,
        squeeze_second,
        expand_weight,
        expand_moment,
        expand_second,
        project_weight,
        project_moment,
        project_second,
    )
    held = (*states, norm_params, norm_moment, norm_second)
    sums = (
        sum1.reshape(BOTTLE, lanes1),
        sumc.reshape(conv_weight.shape),
        sum3,
        sume,
        norm_grads,
    )
    block_out, images_grad, *updated = pl.pallas_call(
        update_kernel,
        out_shape=[
            jax.ShapeDtypeStruct(pixel_form, BF16),
            jax.ShapeDtypeStruct(pixel_form, F32),
            *[jax.ShapeDtypeStruct(state.shape, F32) for state in held],
        ],
        in_specs=[any_space] * 25,
        out_specs=[any_space] * 20,
        scratch_shapes=[vmem(values.shape, F32) for values in (*sums, *held, *held)]
        + [vmem(pixel_form, BF16), vmem(pixel_form, F32)]
        + [dma((2, 3)), dma((23,)), dma((18,))],
        compiler_params=pltpu.CompilerParams(vmem_limit_bytes=63 * 1024 * 1024),
    )(block_out, images_grad, *sums, *held)
    by_image = lambda values: jnp.transpose(
        values.reshape(SIDE, SIDE, images.shape[0], CHANNELS), (2, 0, 1, 3)
    )
    return (
        by_image(block_out),
        by_image(images_grad),
        *updated,
    )


def solution(mesh):
    placed = (
        P(("dp", "rep"), None, None, None),
        P(("dp", "rep"), None, None, None),
        P("dp", None),
        P("dp", None),
        P("dp", None),
        P("dp", None),
        P("dp", None),
        P("dp", None),
        P("dp", None),
        P("dp", None),
        P("dp", None),
        P("dp", None),
        P("dp", None),
        P("dp", None),
        P("dp", None),
        P("dp", None),
        P("dp", None),
        P("dp"),
        P("dp"),
        P("dp"),
    )
    n_dp, n_rep = mesh.shape["dp"], mesh.shape["rep"]
    whole_tiles = n_rep == 4 and n_dp % 2 == 0 and INNER % (16 * n_dp) == 0
    return jax.shard_map(
        fused_device if whole_tiles else per_device,
        mesh=mesh,
        in_specs=placed,
        out_specs=(
            P(("dp", "rep"), None, None, None),
            P(("dp", "rep"), None, None, None),
            P("dp", None),
            P("dp", None),
            P("dp", None),
            P("dp", None),
            P("dp", None),
            P("dp", None),
            P("dp", None),
            P("dp", None),
            P("dp", None),
            P("dp", None),
            P("dp", None),
            P("dp", None),
            P("dp", None),
            P("dp", None),
            P("dp", None),
            P("dp"),
            P("dp"),
            P("dp"),
        ),
        check_vma=False,
    )
```

profile of v0, /device:TPU:0, one launch (start us, length us, event | category | flops | bytes accessed | tf_op | source)
XLA Modules:
  0.0 112.4 jit_solution(9895835286194779613)
XLA Ops:
  0.7 106.2 %shard_map.347 = (bf16[196,4,1024]{2,1,0:T(4,128)(2,1)}, f32[196,4,1024]{2,1,0:T(4,128)}, f32[2,2,64,128]{3,2,1,0:T(8,128)}, f32[2,144,256]{2,1,0:T(8,128)}, f32...) custom-call(bf16[196,4,1024]{2,1,0:T(4,128)(2,1)} %bitcast.14, bf16[196,4,1024]{2,1,0:T(4,128)(2,1)} %bitcast.15, ...), custom_call_target="tpu_custom_call" | custom-call | tf_op jit(solution)/shard_map/pallas_call | solution.py:1576
  106.9 5.5 %shard_map.348 = (bf16[196,4,1024]{2,1,0:T(4,128)(2,1)}, f32[196,4,1024]{2,1,0:T(4,128)}, f32[128,256]{1,0:T(8,128)}, f32[128,256]{1,0:T(8,128)}, f32[128,256]{1...) custom-call(bf16[196,4,1024]{2,1,0:T(4,128)(2,1)} %get-tuple-element, ...), custom_call_target="tpu_custom_call" | custom-call | tf_op jit(solution)/shard_map/pallas_call | solution.py:1625
where the time goes:
time: 113 us; the launch traced here: 112 us
  Pallas kernels  112 us (99%)
    pallas_call x1, Pallas kernels, fused_device(): pl.pallas_call(functools.partial(block_kernel, n_dp, n_rep), out_shape=[j...  106 us
    pallas_call x1, Pallas kernels, fused_device(): pl.pallas_call(update_kernel, out_shape=[jax.ShapeDtypeStruct(pixel_form,...  5.49 us

commit v1 on v0

--- a/solution.py
+++ b/solution.py
@@ -1282,12 +1282,15 @@
         if group == 0:
             reduce_owner(3)
             reduce_owner(4)
-            reduce_y(1)
+    reduce_y(1)
     reduce_y(2)
     sum_turn("back_reduced0")
-    sum_turn("back_reduced1")
     g1[...] = tdot(mixed[...], x_v[...]).reshape(g1.shape)
     reduce_core(0)
+    sum_turn("back_reduced1")
+    reduce_owner(1)
+    reduce_y(0)
+    reduce_owner(2)
     found = [unstack_sums(sum_end(f"back_reduced{group}")) for group in range(2)]
     bias_sum, gain_sum = (jnp.concatenate(item, axis=1) for item in zip(*found))
     write_norm(0, gain_sum)
@@ -1300,9 +1303,7 @@
         return carry
 
     over_rows(make_dred, 0)
-    reduce_owner(1)
     proj[...] = dot_t(dred[...], fw1[...].reshape(CHANNELS, BOTTLE))
-    reduce_y(0)
 
     by_bias = mul1 * bias_sum * (1.0 / pixels)
     by_gain = mul1 * gain_sum * (1.0 / pixels)
@@ -1318,6 +1319,8 @@
         fix[1 + m] = row_dot(by_gain, jnp.where(ids == 2 * m, 1.0, 0.0))
     reduce_spread(3)
     reduce_spread(4)
+    reduce_owner(0)
+    reduce_spread(1)
 
     def make_dx(row, carry):
         for start in range(0, CHANNELS, 256):
@@ -1335,9 +1338,6 @@
         norm_rows = jnp.where(dp == d, np_full[at : at + 8, :], norm_rows)
     norm_rows = pltpu.roll(norm_rows, lax.rem(128 - turn, 128), 1)
     gn_out[...] = jnp.where(lanes_id < 128 - turn, norm_rows, pltpu.roll(norm_rows, 7, 0))
-    reduce_owner(2)
-    reduce_owner(0)
-    reduce_spread(1)
     reduce_spread(2)
     reduce_spread(0)
     out_copies = [

time: 113 us -> 110 us (0.973)
  Pallas kernels: 112 us -> 109 us
    pallas_call x1, Pallas kernels: 106 us -> 104 us  [fused_device(): pl.pallas_call(functools.partial(block_kernel, n_dp, n_rep), out_shape=[j...]
where the time goes in v1:
time: 110 us
  Pallas kernels  109 us (99%)
    pallas_call x1, Pallas kernels, fused_device(): pl.pallas_call(functools.partial(block_kernel, n_dp, n_rep), out_shape=[j...  104 us
    pallas_call x1, Pallas kernels, fused_device(): pl.pallas_call(update_kernel, out_shape=[jax.ShapeDtypeStruct(pixel_form,...  5.49 us

profile of v1, /device:TPU:0, one launch (start us, length us, event | category | flops | bytes accessed | tf_op | source)
XLA Modules:
  0.0 110.1 jit_solution(2837319736482712274)
XLA Ops:
  0.7 104.0 %shard_map.347 = (bf16[196,4,1024]{2,1,0:T(4,128)(2,1)}, f32[196,4,1024]{2,1,0:T(4,128)}, f32[2,2,64,128]{3,2,1,0:T(8,128)}, f32[2,144,256]{2,1,0:T(8,128)}, f32...) custom-call(bf16[196,4,1024]{2,1,0:T(4,128)(2,1)} %bitcast.14, bf16[196,4,1024]{2,1,0:T(4,128)(2,1)} %bitcast.15, ...), custom_call_target="tpu_custom_call" | custom-call | tf_op jit(solution)/shard_map/pallas_call | solution.py:1576
  104.6 5.5 %shard_map.348 = (bf16[196,4,1024]{2,1,0:T(4,128)(2,1)}, f32[196,4,1024]{2,1,0:T(4,128)}, f32[128,256]{1,0:T(8,128)}, f32[128,256]{1,0:T(8,128)}, f32[128,256]{1...) custom-call(bf16[196,4,1024]{2,1,0:T(4,128)(2,1)} %get-tuple-element, ...), custom_call_target="tpu_custom_call" | custom-call | tf_op jit(solution)/shard_map/pallas_call | solution.py:1625

commit v2 on v1

--- a/solution.py
+++ b/solution.py
@@ -745,8 +745,6 @@
         dcol[0:PAD, lane_block * 256 : lane_block * 256 + 256] = zero_rows
         dcol[PAD + ROWS : 2 * PAD + ROWS, lane_block * 256 : lane_block * 256 + 256] = zero_rows
     gather_hand(0)
-    gather_out(2)
-    gather_out(3)
     gather_turn(1)
 
     def sum_start(k, payload):
@@ -925,7 +923,8 @@
         return unstack_sums(unfold_lanes(sum_end(name)))
 
     sum_start("reduced", joined([sums_of(red, 0, 256)]))
-    gather_turn(2)
+    gather_out(2)
+    gather_out(3)
 
     gy_copy.wait()
     to_rows(gy4, gy_v)
@@ -955,7 +954,7 @@
 
     over_rows(make_active, 0)
     gather_hand(1)
-    gather_hand(2)
+    gather_turn(2)
     gather_turn(3)
     place = lax.rem(lax.broadcasted_iota(jnp.int32, (CHUNK, BOTTLE), 0) // 4, SIDE)
     not_last = place != SIDE - 1
@@ -993,6 +992,7 @@
         sum_start(f"widened{group}", joined([sums_of(wid, group * 256, 256)]))
     sum_turn("widened0")
     sum_turn("widened1")
+    gather_hand(2)
     gather_hand(3)
 
     norm2 = []

time: 110 us -> 109 us (level)
  no operation moved by 1% of the time
where the time goes in v2:
time: 109 us
  Pallas kernels  108 us (99%)
    pallas_call x1, Pallas kernels, fused_device(): pl.pallas_call(functools.partial(block_kernel, n_dp, n_rep), out_shape=[j...  103 us
    pallas_call x1, Pallas kernels, fused_device(): pl.pallas_call(update_kernel, out_shape=[jax.ShapeDtypeStruct(pixel_form,...  5.49 us

profile of v2, /device:TPU:0, one launch (start us, length us, event | category | flops | bytes accessed | tf_op | source)
XLA Modules:
  0.0 109.1 jit_solution(5279957879179461720)
XLA Ops:
  0.7 102.9 %shard_map.347 = (bf16[196,4,1024]{2,1,0:T(4,128)(2,1)}, f32[196,4,1024]{2,1,0:T(4,128)}, f32[2,2,64,128]{3,2,1,0:T(8,128)}, f32[2,144,256]{2,1,0:T(8,128)}, f32...) custom-call(bf16[196,4,1024]{2,1,0:T(4,128)(2,1)} %bitcast.14, bf16[196,4,1024]{2,1,0:T(4,128)(2,1)} %bitcast.15, ...), custom_call_target="tpu_custom_call" | custom-call | tf_op jit(solution)/shard_map/pallas_call | solution.py:1576
  103.6 5.5 %shard_map.348 = (bf16[196,4,1024]{2,1,0:T(4,128)(2,1)}, f32[196,4,1024]{2,1,0:T(4,128)}, f32[128,256]{1,0:T(8,128)}, f32[128,256]{1,0:T(8,128)}, f32[128,256]{1...) custom-call(bf16[196,4,1024]{2,1,0:T(4,128)(2,1)} %get-tuple-element, ...), custom_call_target="tpu_custom_call" | custom-call | tf_op jit(solution)/shard_map/pallas_call | solution.py:1625

commit v3 on v2

--- a/solution.py
+++ b/solution.py
@@ -955,7 +955,6 @@
     over_rows(make_active, 0)
     gather_hand(1)
     gather_turn(2)
-    gather_turn(3)
     place = lax.rem(lax.broadcasted_iota(jnp.int32, (CHUNK, BOTTLE), 0) // 4, SIDE)
     not_last = place != SIDE - 1
     not_first = place != 0
@@ -993,7 +992,7 @@
     sum_turn("widened0")
     sum_turn("widened1")
     gather_hand(2)
-    gather_hand(3)
+    gather_turn(3)
 
     norm2 = []
     pooled = jnp.zeros((8, BOTTLE), F32)
@@ -1022,6 +1021,8 @@
     )
     pre_pool = exact_dot(pooled, squeeze, False)
     sum_start("pool", stack_sums(pair_sum(pre_pool), pair_sum(pre_pool * pre_pool)))
+    gather_hand(3)
+
     first_micro = lax.rem(row_ids(BOTTLE), 4) < 2
 
     def make_normed(row, carry):

time: 109 us -> 109 us (level)
  no operation moved by 1% of the time
where the time goes in v3:
time: 109 us; the launch traced here: 108 us
  Pallas kernels  108 us (99%)
    pallas_call x1, Pallas kernels, fused_device(): pl.pallas_call(functools.partial(block_kernel, n_dp, n_rep), out_shape=[j...  102 us
    pallas_call x1, Pallas kernels, fused_device(): pl.pallas_call(update_kernel, out_shape=[jax.ShapeDtypeStruct(pixel_form,...  5.49 us

profile of v3, /device:TPU:0, one launch (start us, length us, event | category | flops | bytes accessed | tf_op | source)
XLA Modules:
  0.0 108.5 jit_solution(18378268362117807444)
XLA Ops:
  0.7 102.3 %shard_map.347 = (bf16[196,4,1024]{2,1,0:T(4,128)(2,1)}, f32[196,4,1024]{2,1,0:T(4,128)}, f32[2,2,64,128]{3,2,1,0:T(8,128)}, f32[2,144,256]{2,1,0:T(8,128)}, f32...) custom-call(bf16[196,4,1024]{2,1,0:T(4,128)(2,1)} %bitcast.14, bf16[196,4,1024]{2,1,0:T(4,128)(2,1)} %bitcast.15, ...), custom_call_target="tpu_custom_call" | custom-call | tf_op jit(solution)/shard_map/pallas_call | solution.py:1577
  103.0 5.5 %shard_map.348 = (bf16[196,4,1024]{2,1,0:T(4,128)(2,1)}, f32[196,4,1024]{2,1,0:T(4,128)}, f32[128,256]{1,0:T(8,128)}, f32[128,256]{1,0:T(8,128)}, f32[128,256]{1...) custom-call(bf16[196,4,1024]{2,1,0:T(4,128)(2,1)} %get-tuple-element, ...), custom_call_target="tpu_custom_call" | custom-call | tf_op jit(solution)/shard_map/pallas_call | solution.py:1626
